TPU v7x, 32 devices: a whole 2x2x4 slice. The times are simulated.
32 devices in a mesh: ctx: 8 (over z, y), tp: 4 (over x, core).
Axes of the slice: x: 2, y: 2, z: 4, core: 2. Of those that a mesh axis runs over, the one named last changes fastest.
Arguments:
- features: bfloat16 [1024, 3, 4096], P('ctx', None, 'tp'), may hold values from -6 to 6
- short_taps: float32 [3, 3, 4096], P(None, None, 'tp'), may hold values from -3 to 3
- residues: float32 [16, 4096], P(None, 'tp'), may hold values from -2 to 2
- log_rate: float32 [16, 4096], P(None, 'tp'), may hold values from -13 to -3.5, as said below
- out_weight: bfloat16 [4096, 8192], P('tp'), may hold values from -0.09375 to 0.09375
- grad_out: bfloat16 [1024, 8192], P('ctx', 'tp'), may hold values from -6 to 6
Outputs:
- grad_features: bfloat16 [1024, 3, 4096], P('ctx', None, 'tp')
- grad_taps: float32 [3, 3, 4096], P(None, None, 'tp')
- grad_residues: float32 [16, 4096], P(None, 'tp')
- grad_log_rate: float32 [16, 4096], P(None, 'tp')
- grad_weight_t: float32 [8192, 4096], P('ctx', 'tp')
Inputs may be any that keep to these rules, and one draw needn't show every extreme that they name: `log_rate`: log of a decay rate per token.
All inputs are finite; a program needn't handle non-finite values.
Results may differ from a plain program's by a relative error of at most 0.0058.
Values may be sent and summed in bfloat16 or wider, within the bound.
A program may use at most 192 MiB of HBM per device.

v0:
```python
import jax
import jax.numpy as jnp
from jax import lax
from jax.sharding import PartitionSpec as P


def shifted(value, axis, steps):
    count = lax.axis_size(axis)
    first, last = (max(0, -steps), min(count, count - steps))
    return lax.ppermute(value, axis, [(source, source + steps) for source in range(first, last)])


def block_tables(residues, log_rate, block_len):
    decay_rate = jnp.exp(log_rate)
    amplitude = residues * jnp.exp(0.5 * log_rate)
    lag_steps = jnp.arange(block_len).astype(jnp.float32)
    kernel = jnp.sum(
        amplitude[:, None, :] * jnp.exp(-decay_rate[:, None, :] * lag_steps[None, :, None]), axis=0
    )
    row_ids = jnp.arange(block_len)[:, None]
    col_ids = jnp.arange(block_len)[None, :]
    distance = row_ids - col_ids
    toeplitz = jnp.where((distance >= 0)[:, :, None], kernel[jnp.maximum(distance, 0)], 0.0)
    injection = jnp.exp(-decay_rate[:, None, :] * (block_len - 1 - lag_steps)[None, :, None])
    readout = amplitude[:, None, :] * jnp.exp(
        -decay_rate[:, None, :] * (lag_steps + 1.0)[None, :, None]
    )
    return (decay_rate, toeplitz, injection, readout)


def combine_states(earlier, later):
    return (earlier[0] * later[0], later[0] * earlier[1] + later[1])


def long_conv(product, residues, log_rate):
    block_len = 128
    length, channels = product.shape
    block_count = length // block_len
    decay_rate, toeplitz, injection, readout = block_tables(residues, log_rate, block_len)
    blocks = product.reshape(block_count, block_len, channels)
    inside = jnp.einsum("ijc,bjc->bic", toeplitz, blocks, precision=lax.Precision.HIGHEST)
    entering = jnp.einsum("rjc,bjc->brc", injection, blocks, precision=lax.Precision.HIGHEST)
    carry_decay = jnp.broadcast_to(jnp.exp(-decay_rate * block_len), entering.shape)
    unused, states = lax.associative_scan(combine_states, (carry_decay, entering), axis=0)
    before = jnp.concatenate([jnp.zeros_like(states[:1]), states[:-1]], axis=0)
    from_past = jnp.einsum("ric,brc->bic", readout, before, precision=lax.Precision.HIGHEST)
    return (inside + from_past).reshape(length, channels)


def to_channels(values):
    return lax.all_to_all(values, "ctx", split_axis=1, concat_axis=0, tiled=True)


def to_tokens(values):
    return lax.all_to_all(values, "ctx", split_axis=0, concat_axis=1, tiled=True)


def per_device(features, short_taps, residues, log_rate, out_weight, grad_out):
    length = features.shape[0]
    tap_count = short_taps.shape[0]
    groups = lax.axis_size("ctx")
    position = lax.axis_index("ctx")
    rim_rows = shifted(features[length - (tap_count - 1) :], "ctx", 1)
    padded_in = jnp.concatenate([rim_rows, features], axis=0).astype(jnp.float32)
    shortened = sum(
        (
            short_taps[lag] * padded_in[tap_count - 1 - lag : tap_count - 1 - lag + length]
            for lag in range(tap_count)
        )
    )
    product = (shortened[:, 1] * shortened[:, 2]).astype(jnp.bfloat16)
    chan_width = product.shape[1] // groups
    local_residues = lax.dynamic_slice_in_dim(residues, position * chan_width, chan_width, 1)
    local_rates = lax.dynamic_slice_in_dim(log_rate, position * chan_width, chan_width, 1)
    product_chan = to_channels(product).astype(jnp.float32)
    conv_chan, pullback = jax.vjp(long_conv, product_chan, local_residues, local_rates)
    convolved = to_tokens(conv_chan.astype(jnp.bfloat16)).astype(jnp.float32)
    gated = (shortened[:, 0] * convolved).astype(jnp.bfloat16)
    cotangent = lax.all_gather(grad_out, "tp", axis=1, tiled=True)
    grad_weight_t = lax.psum_scatter(
        lax.dot_general(
            cotangent, gated, (((0,), (0,)), ((), ())), preferred_element_type=jnp.float32
        ),
        "ctx",
        scatter_dimension=0,
        tiled=True,
    )
    grad_gated = lax.dot_general(
        cotangent, out_weight, (((1,), (1,)), ((), ())), preferred_element_type=jnp.float32
    )
    grad_conv = (grad_gated * shortened[:, 0]).astype(jnp.bfloat16)
    grad_prod_chan, grad_res_local, grad_rate_local = pullback(
        to_channels(grad_conv).astype(jnp.float32)
    )
    grad_product = to_tokens(grad_prod_chan.astype(jnp.bfloat16)).astype(jnp.float32)
    grad_residues, grad_log_rate = (
        lax.all_gather(grad_res_local, "ctx", axis=1, tiled=True),
        lax.all_gather(grad_rate_local, "ctx", axis=1, tiled=True),
    )
    grad_short = jnp.stack(
        [grad_gated * convolved, grad_product * shortened[:, 2], grad_product * shortened[:, 1]],
        axis=1,
    )
    tail_rows = shifted(grad_short[: tap_count - 1], "ctx", -1)
    tail_pad = jnp.concatenate([grad_short, tail_rows], axis=0)
    grad_features = sum(
        (short_taps[lag] * tail_pad[lag : lag + length] for lag in range(tap_count))
    )
    partial_taps = jnp.stack(
        [
            jnp.sum(
                grad_short * padded_in[tap_count - 1 - lag : tap_count - 1 - lag + length], axis=0
            )
            for lag in range(tap_count)
        ],
        axis=0,
    )
    grad_taps = lax.psum(partial_taps, "ctx")
    return (
        grad_features.astype(jnp.bfloat16),
        grad_taps,
        grad_residues,
        grad_log_rate,
        grad_weight_t,
    )


def solution(mesh):
    return jax.shard_map(
        per_device,
        mesh=mesh,
        in_specs=(
            P("ctx", None, "tp"),
            P(None, None, "tp"),
            P(None, "tp"),
            P(None, "tp"),
            P("tp", None),
            P("ctx", "tp"),
        ),
        out_specs=(
            P("ctx", None, "tp"),
            P(None, None, "tp"),
            P(None, "tp"),
            P(None, "tp"),
            P("ctx", "tp"),
        ),
        check_vma=False,
    )
```

profile of v0, /device:TPU:0, one launch (start us, length us, event | category | flops | bytes accessed | tf_op | source)
XLA Modules:
  0.0 879.5 jit_solution(6375209423134570061)
XLA Ops:
  7.9 0.8 slice.128
  8.7 4.9 collective-permute-start
  15.0 0.8 slice_bitcast_fusion.3
  16.3 1.4 maximum_convert_fusion
  18.2 0.8 multiply_convert_fusion.2
  18.9 1.8 copy.151
  20.7 5.3 all-to-all-start
  26.6 0.7 copy.122
  28.0 6.5 all-to-all-done
  34.5 2.8 fusion.16
  37.4 1.2 copy.128
  38.6 13.0 %multiply_convert_fusion.1 = (bf16[128,1024]{1,0:T(8,128)(2,1)}, f32[128,1024]{1,0:T(8,128)}) fusion(f32[128,3,1024]{2,0,1:T(8,128)S(1)} %multiply_add_fusion, bf16[128,8192]{1,0:T(8,128)(2,1)} %all-gather.2.cloned.1.call-done, bf16[1024,8192]{1,0:T(8,128)(2,1)} %param.10), kind=kOutput, calls=%fused_computation.43 | convolution fusion | flops 2147745792 | bytes 20185088 | tf_op jit(solution)/shard_map/dot_general | solution.py:88
  51.6 1.8 copy.153
  53.4 4.1 all-to-all-start.2
  60.4 3.2 pad.240
  63.6 2.0 all-to-all-done.2
  65.7 3.0 fusion.11
  68.7 1.8 copy.134
  70.6 0.8 split.20
  72.0 1.3 pad_maximum_fusion.3
  73.3 1.8 pad.157
  75.2 0.9 slice_add_fusion.6
  76.0 1.0 copy.156
  77.0 3.3 fusion.13
  80.3 5.6 select_bitcast_fusion
  85.9 9.3 %copy.155 = f32[128,128,128]{2,1,0:T(8,128)} copy(f32[128,128,128]{1,0,2:T(8,128)} %select_bitcast_fusion) | data formatting | bytes 16777216 | tf_op jit(solution)/shard_map/transpose(jvp(jit(_where)))/select_n | solution.py:23
  95.2 98.8 %scatter_custom_fusion = f32[128,128]{1,0:T(8,128)S(1)} fusion(s32[16384]{0:T(1024)} %maximum_bitcast_fusion, f32[16384,128]{1,0:T(8,128)} %bitcast.83, f32[]{:T(128)} %constant.7.clone.1), kind=kCustom, calls=%fused_computation.85 | custom fusion | flops 2097152 | bytes 66048 | tf_op jit(solution)/shard_map/transpose(jvp())/scatter-add | solution.py:23
  194.8 4.6 multiply_reduce_fusion.4
  199.4 0.9 copy.124
  200.3 54.8 %gather_fusion = f32[16384,128]{1,0:T(8,128)} fusion(f32[128,128]{1,0:T(8,128)S(1)} %copy.124, s32[16384]{0:T(1024)S(1)} %broadcast_clamp_fusion), kind=kCustom, calls=%fused_computation | custom fusion | bytes 16842752 | tf_op jit(solution)/shard_map/jvp()/gather | solution.py:23
  255.1 9.9 %broadcast_select_fusion = f32[128,128,128]{2,1,0:T(8,128)} fusion(f32[128,128,128]{2,1,0:T(8,128)} %bitcast.82, pred[128,128]{1,0:T(8,128)(4,1)} %subtract_compare_fusion), kind=kLoop, calls=%fused_computation.4 | loop fusion | flops 2097152 | bytes 16793600 | tf_op jit(solution)/shard_map/jvp(jit(_where))/select_n | solution.py:23
  265.1 9.3 %copy.126 = f32[128,128,128]{1,0,2:T(8,128)} copy(f32[128,128,128]{2,1,0:T(8,128)} %broadcast_select_fusion) | data formatting | bytes 16777216 | tf_op jit(solution)/shard_map/jvp(jit(_where))/select_n | solution.py:23
  274.3 10.1 %fusion.9 = bf16[8,128,128]{1,0,2:T(8,128)(2,1)S(1)} fusion(f32[128,8,128]{2,1,0:T(8,128)} %fusion.13, f32[128,128,128]{1,0,2:T(8,128)} %copy.126, bf16[128,8,128]{0,2,1:T(8,128)(2,1)} %all-to-all-done), kind=kOutput, calls=%fused_computation.26 | convolution fusion | flops 201588736 | bytes 9437184 | tf_op jit(solution)/shard_map/jvp(ijc,bjc->bic)/dot_general | solution.py:41
  284.5 12.0 %all_to_all.43 = bf16[8,128,128]{1,2,0:T(8,128)(2,1)S(1)} all-to-all(bf16[8,128,128]{1,2,0:T(8,128)(2,1)S(1)} %copy.130), channel_id=1, replica_groups=mesh['ctx'=8,'tp'=4] {'ctx'}, dimensions={0} | all-to-all | bytes 524288 | tf_op jit(solution)/shard_map/all_to_all | solution.py:55
  296.5 0.8 convert_element_type.103
  297.3 2.0 copy.152
  299.4 17.4 %convolution_bitcast_fusion = f32[8192,1024]{0,1:T(8,128)} fusion(bf16[128,8192]{1,0:T(8,128)(2,1)} %all-gather.2.cloned.1.call-done, f32[128,1024]{1,0:T(8,128)} %copy.152, f32[128,3,1024]{2,0,1:T(8,128)S(1)} %multiply_add_fusion), kind=kOutput, calls=%fused_computation.2 | convolution fusion | flops 2147745792 | bytes 36700160 | tf_op jit(solution)/shard_map/dot_general | solution.py:81
  316.8 1.3 split.21
  320.3 1.9 pad.134
  322.2 1.4 multiply_add_fusion.1
  323.8 2.6 pad.113
  326.4 0.9 add_bitcast_fusion
  327.3 1.0 copy.135
  328.3 2.2 fusion.15
  330.5 7.5 fusion.8
  338.0 0.7 copy.137
  338.7 4.1 all-to-all-start.3
  342.8 3.3 fusion.5
  346.2 0.9 copy.148
  347.1 0.9 copy.145
  348.0 0.9 copy.143
  349.0 0.9 copy.144
  349.9 0.9 copy.149
  350.8 0.7 multiply_add_fusion.3
  351.6 32.6 %all_gather.11 = f32[16,1024]{1,0:T(8,128)S(1)} all-gather(f32[16,128]{1,0:T(8,128)S(1)} %get-tuple-element.56), channel_id=1, replica_groups=mesh['ctx'=8,'tp'=4] {'ctx'}, dimensions={1}, use_global_device_ids=true | all-gather | bytes 73728 | tf_op jit(solution)/shard_map/all_gather | solution.py:98
  384.2 1.8 convert_element_type.104
  386.0 2.0 copy.154
  388.0 1.3 multiply_bitcast_fusion
  389.6 1.3 collective-permute-start.1
  391.0 32.0 %all_gather.10 = f32[16,1024]{1,0:T(8,128)S(1)} all-gather(f32[16,128]{1,0:T(8,128)S(1)} %get-tuple-element.57), channel_id=1, replica_groups=mesh['ctx'=8,'tp'=4] {'ctx'}, dimensions={1}, use_global_device_ids=true | all-gather | bytes 73728 | tf_op jit(solution)/shard_map/all_gather | solution.py:97
  423.2 1.9 multiply_reduce_fusion.2
  425.1 40.6 %psum.7 = f32[3,3,1024]{2,1,0:T(4,128)} all-reduce(f32[3,3,1024]{2,1,0:T(4,128)S(1)} %pad_maximum_fusion.2), channel_id=1, replica_groups=mesh['ctx'=8,'tp'=4] {'ctx'}, use_global_device_ids=true, to_apply=%region_4.5 | all-reduce | flops 9216 | bytes 73728 | tf_op jit(solution)/shard_map/psum | solution.py:118
  465.8 400.1 %reduce-scatter.2.cloned.1.call-done = f32[1024,1024]{0,1:T(8,128)} async-done(((f32[8192,1024]{0,1:T(8,128)}), f32[1024,1024]{0,1:T(8,128)}) %reduce-scatter.2.cloned.1.call-update) | async-done | bytes 4194320 | tf_op jit(solution)/shard_map/reduce_scatter | solution.py:80
  865.8 5.3 copy.150
  (103 shorter events, 12.7 us)
Async XLA Ops:
  7.2 31.5 %all-gather.2.cloned.1.call-start = ((), (), s32[]{:S(2)}) async-start(), calls=%async_computation.5 | async-start | bytes 2621440 | tf_op jit(solution)/shard_map/all_gather | solution.py:79
  8.7 7.6 collective-permute-start
  13.6 20.9 %copy-start.20 = (f32[128]{0:T(128)}, f32[128]{0:T(128)S(1)}, u32[]{:S(2)}) copy-start(f32[128]{0:T(128)S(1)} %broadcast_subtract_fusion) | copy-start | bytes 1540
  15.0 23.6 %copy-start.15 = (f32[16,128]{1,0:T(8,128)}, f32[16,128]{1,0:T(8,128)S(1)}, u32[]{:S(2)}) copy-start(f32[16,128]{1,0:T(8,128)S(1)} %get-tuple-element.51) | copy-start | bytes 24580
  15.8 2.4 copy-start.3
  15.8 2.4 copy-start.5
  15.8 2.4 copy-start.7
  20.7 13.8 %all-to-all-start = ((bf16[128,8,128]{0,2,1:T(8,128)(2,1)}), bf16[128,8,128]{0,2,1:T(8,128)(2,1)}, u32[]{:S(2)}, u32[]{:S(2)}) async-start(bf16[128,8,128]{0,2,1:T(8,128)(2,1)} %bitcast.87), calls=%async_computation | async-start | bytes 524288 | tf_op jit(solution)/shard_map/all_to_all | solution.py:51
  38.6 19.2 %copy-start.17 = (f32[2,16,128]{2,1,0:T(8,128)}, f32[2,16,128]{2,1,0:T(8,128)S(1)}, u32[]{:S(2)}) copy-start(f32[2,16,128]{2,1,0:T(8,128)S(1)} %slice_add_fusion.3) | copy-start | bytes 49156
  53.4 12.3 %all-to-all-start.2 = ((bf16[128,8,128]{0,2,1:T(8,128)(2,1)}), bf16[128,8,128]{0,2,1:T(8,128)(2,1)}, u32[]{:S(2)}, u32[]{:S(2)}) async-start(bf16[128,8,128]{0,2,1:T(8,128)(2,1)} %bitcast.86), calls=%async_computation.2 | async-start | bytes 524288 | tf_op jit(solution)/shard_map/all_to_all | solution.py:51
  57.5 808.4 %reduce-scatter.2.cloned.1.call-start = ((), (), s32[]{:S(2)}) async-start(), calls=%async_computation.6 | async-start | bytes 37748736 | tf_op jit(solution)/shard_map/reduce_scatter | solution.py:80
  57.8 0.6 copy-start.11
  57.8 0.6 copy-start.13
  71.4 2.0 copy-start.10
  77.0 3.3 copy-start.2
  316.8 1.4 copy-start.1
  316.8 1.4 copy-start.12
  316.8 1.4 copy-start.14
  316.8 2.0 copy-start.18
  316.8 2.0 copy-start.16
  316.8 2.0 copy-start.22
  330.5 12.3 %copy-start.21 = (f32[128]{0:T(128)S(1)}, f32[128]{0:T(128)}, u32[]{:S(2)}) copy-start(f32[128]{0:T(128)} %copy-done.20) | copy-start | bytes 1540
  338.0 8.2 copy-start.19
  338.0 8.2 copy-start.9
  338.7 45.5 %all-to-all-start.3 = ((bf16[8,128,128]{1,2,0:T(8,128)(2,1)}), bf16[8,128,128]{1,2,0:T(8,128)(2,1)}, u32[]{:S(2)}, u32[]{:S(2)}) async-start(bf16[8,128,128]{1,2,0:T(8,128)(2,1)} %copy.137), calls=%async_computation.3 | async-start | bytes 524288 | tf_op jit(solution)/shard_map/all_to_all | solution.py:55
  388.0 1.4 copy-start
  389.6 33.3 %collective-permute-start.1 = (f32[2,3,1024]{2,0,1:T(2,128)S(1)}, f32[2,3,1024]{2,0,1:T(2,128)S(1)}, u32[]{:S(2)}, u32[]{:S(2)}) collective-permute-start(f32[2,3,1024]{2,0,1:T(2,128)S(1)} %slice.179), channel_id=1, source_target_pairs={{4,0},{8,4},{12,8},{16,12},{20,16},{24,20},{28,24},{5,1},{9,5},{13... | collective-permute-start | bytes 73736 | tf_op jit(solution)/shard_map/ppermute | solution.py:10
  390.9 32.3 %copy-start.4 = (f32[3,1024]{1,0:T(4,128)S(1)}, f32[3,1024]{1,0:T(4,128)}, u32[]{:S(2)}) copy-start(f32[3,1024]{1,0:T(4,128)} %copy-done.3) | copy-start | bytes 36868
  390.9 32.3 %copy-start.6 = (f32[3,1024]{1,0:T(4,128)S(1)}, f32[3,1024]{1,0:T(4,128)}, u32[]{:S(2)}) copy-start(f32[3,1024]{1,0:T(4,128)} %copy-done.5) | copy-start | bytes 36868
  390.9 32.3 %copy-start.8 = (f32[3,1024]{1,0:T(4,128)S(1)}, f32[3,1024]{1,0:T(4,128)}, u32[]{:S(2)}) copy-start(f32[3,1024]{1,0:T(4,128)} %copy-done.7) | copy-start | bytes 36868
Sparse Core Ops, SparseCore 0:
  9.6 25.2 all-gather.1
  317.0 548.8 reduce-scatter.1
where the time goes:
time: 888 us; the launch traced here: 879 us
  waiting for transfers between devices  409 us (46%)
  other arithmetic  129 us (15%)
  blocking collectives  117 us (13%)
  local copies, waits for them, and re-layouts  116 us (13%)
  matrix products  72.8 us (8%)
  starting transfers between devices  20 us (2%)
  between operations  14.8 us (2%)
    reduce_scatter x1, waiting for transfers between devices, per_device(): lax.psum_scatter(lax.dot_general(cotangent, gated, (((0,), (0,)), ((), ()...  400 us
    scatter-add x1, other arithmetic, block_tables(): kernel[jnp.maximum(distance, 0)]  98.8 us
    gather x1, local copies, waits for them, and re-layouts, block_tables(): kernel[jnp.maximum(distance, 0)]  54.8 us
    psum x1, blocking collectives, per_device(): grad_taps = lax.psum(partial_taps, 'ctx')  40.6 us
    all_gather x1, blocking collectives, per_device(): lax.all_gather(grad_rate_local, 'ctx', axis=1, tiled=True)  32.6 us
    all_gather x1, blocking collectives, per_device(): lax.all_gather(grad_res_local, 'ctx', axis=1, tiled=True)  32 us
    dot_general x3, matrix products, long_conv(): jnp.einsum('ijc,bjc->bic', toeplitz, blocks, precision=lax.Precision.HIGH...  23.2 us
    select_n x2, local copies, waits for them, and re-layouts, block_tables(): jnp.where((distance >= 0)[:, :, None], kernel[jnp.maximum(distance, 0)],...  18.6 us
  transfers between devices with their start and end apart: 7, of which 3 were waited for; matrix products, arithmetic and copies ran while one was open for 7% of the time, Pallas kernels for 0%

commit v1 on v0

--- a/solution.py
+++ b/solution.py
@@ -2,6 +2,23 @@
 import jax.numpy as jnp
 from jax import lax
 from jax.sharding import PartitionSpec as P
+
+
+def joined_along(parts, dim):
+    parts = jnp.moveaxis(parts, 0, dim)
+    shape = parts.shape
+    return parts.reshape(*shape[:dim], shape[dim] * shape[dim + 1], *shape[dim + 2 :])
+
+
+def gather_around(x, axis, dim):
+    size = lax.axis_size(axis)
+    right = [(i, (i + 1) % size) for i in range(size)]
+    blocks = [x]
+    while len(blocks) < size:
+        blocks.append(lax.ppermute(blocks[-1], axis, right))
+    place = lax.axis_index(axis)
+    blocks = jnp.stack(blocks)[(place - jnp.arange(size)) % size]
+    return joined_along(blocks, dim)
 
 
 def shifted(value, axis, steps):
@@ -95,7 +112,7 @@
     grad_product = to_tokens(grad_prod_chan.astype(jnp.bfloat16)).astype(jnp.float32)
     grad_residues, grad_log_rate = (
         lax.all_gather(grad_res_local, "ctx", axis=1, tiled=True),
-        lax.all_gather(grad_rate_local, "ctx", axis=1, tiled=True),
+        gather_around(grad_rate_local, "ctx", 1),
     )
     grad_short = jnp.stack(
         [grad_gated * convolved, grad_product * shortened[:, 2], grad_product * shortened[:, 1]],

time: 888 us -> 888 us (level)
  blocking collectives: 117 us -> 80.9 us
  waiting for transfers between devices: 409 us -> 429 us
  local copies, waits for them, and re-layouts: 116 us -> 125 us
    ppermute x0 -> x7, waiting for transfers between devices: none -> 44.5 us  [gather_around(): blocks.append(lax.ppermute(blocks[-1], axis, right))]
    all_gather x1 -> x0, blocking collectives: 32.6 us -> none  [per_device(): lax.all_gather(grad_rate_local, 'ctx', axis=1, tiled=True)]
    reduce_scatter x1, waiting for transfers between devices: 400 us -> 372 us  [per_device(): lax.psum_scatter(lax.dot_general(cotangent, gated, (((0,), (0,)), ((), ()...]
  transfers between devices with their start and end apart: 7 -> 14, of which waited for: 3 -> 10; matrix products, arithmetic and copies ran while one was open for 7% -> 8% of each run, Pallas kernels for 0% -> 0%
where the time goes in v1:
time: 888 us; the launch traced here: 880 us
  waiting for transfers between devices  429 us (48%)
  other arithmetic  133 us (15%)
  local copies, waits for them, and re-layouts  125 us (14%)
  blocking collectives  80.9 us (9%)
  matrix products  72.9 us (8%)
  starting transfers between devices  24 us (3%)
  between operations  14.8 us (2%)
    reduce_scatter x1, waiting for transfers between devices, per_device(): lax.psum_scatter(lax.dot_general(cotangent, gated, (((0,), (0,)), ((), ()...  372 us
    scatter-add x1, other arithmetic, block_tables(): kernel[jnp.maximum(distance, 0)]  98.8 us
    gather x1, local copies, waits for them, and re-layouts, block_tables(): kernel[jnp.maximum(distance, 0)]  54.4 us
    ppermute x7, waiting for transfers between devices, gather_around(): blocks.append(lax.ppermute(blocks[-1], axis, right))  44.5 us
    psum x1, blocking collectives, per_device(): grad_taps = lax.psum(partial_taps, 'ctx')  36.6 us
    all_gather x1, blocking collectives, per_device(): lax.all_gather(grad_res_local, 'ctx', axis=1, tiled=True)  32.2 us
    dot_general x3, matrix products, long_conv(): jnp.einsum('ijc,bjc->bic', toeplitz, blocks, precision=lax.Precision.HIGH...  23.3 us
    select_n x2, local copies, waits for them, and re-layouts, block_tables(): jnp.where((distance >= 0)[:, :, None], kernel[jnp.maximum(distance, 0)],...  18.6 us
  transfers between devices with their start and end apart: 14, of which 10 were waited for; matrix products, arithmetic and copies ran while one was open for 8% of the time, Pallas kernels for 0%

profile of v1, /device:TPU:0, one launch (start us, length us, event | category | flops | bytes accessed | tf_op | source)
XLA Modules:
  0.0 879.6 jit_solution(17515328480070486467)
XLA Ops:
  8.7 4.9 collective-permute-start
  16.4 1.4 maximum_convert_fusion
  19.0 1.8 copy.207
  20.8 5.2 all-to-all-start
  28.1 6.5 all-to-all-done
  34.6 2.8 fusion.16
  37.5 1.2 copy.183
  38.7 13.0 %multiply_convert_fusion.1 = (bf16[128,1024]{1,0:T(8,128)(2,1)}, f32[128,1024]{1,0:T(8,128)}) fusion(f32[128,3,1024]{2,0,1:T(8,128)S(1)} %multiply_add_fusion, bf16[128,8192]{1,0:T(8,128)(2,1)} %all-gather.2.cloned.1.call-done, bf16[1024,8192]{1,0:T(8,128)(2,1)} %param.10), kind=kOutput, calls=%fused_computation.44 | convolution fusion | flops 2147745792 | bytes 20185088 | tf_op jit(solution)/shard_map/dot_general | solution.py:105
  51.7 1.8 copy.209
  53.5 4.0 all-to-all-start.2
  60.5 3.2 pad.242
  63.7 2.1 all-to-all-done.2
  65.8 3.0 fusion.11
  68.8 1.8 copy.189
  72.1 1.3 pad_maximum_fusion.3
  73.4 1.8 pad.158
  76.1 1.0 copy.212
  77.1 3.3 fusion.13
  80.4 5.6 select_bitcast_fusion
  86.0 9.3 %copy.211 = f32[128,128,128]{2,1,0:T(8,128)} copy(f32[128,128,128]{1,0,2:T(8,128)} %select_bitcast_fusion) | data formatting | bytes 16777216 | tf_op jit(solution)/shard_map/transpose(jvp(jit(_where)))/select_n | solution.py:40
  95.3 98.8 %scatter_custom_fusion = f32[128,128]{1,0:T(8,128)S(1)} fusion(s32[16384]{0:T(1024)} %maximum_bitcast_fusion, f32[16384,128]{1,0:T(8,128)} %bitcast.107, f32[]{:T(128)} %constant.20.clone.1), kind=kCustom, calls=%fused_computation.87 | custom fusion | flops 2097152 | bytes 66048 | tf_op jit(solution)/shard_map/transpose(jvp())/scatter-add | solution.py:40
  194.9 4.6 multiply_reduce_fusion.4
  199.5 0.9 copy.179
  200.4 54.4 %gather_fusion = f32[16384,128]{1,0:T(8,128)} fusion(f32[128,128]{1,0:T(8,128)S(1)} %copy.179, s32[16384]{0:T(1024)S(1)} %broadcast_clamp_fusion), kind=kCustom, calls=%fused_computation | custom fusion | bytes 16842752 | tf_op jit(solution)/shard_map/jvp()/gather | solution.py:40
  254.8 9.9 %broadcast_select_fusion = f32[128,128,128]{2,1,0:T(8,128)} fusion(f32[128,128,128]{2,1,0:T(8,128)} %bitcast.106, pred[128,128]{1,0:T(8,128)(4,1)} %subtract_compare_fusion), kind=kLoop, calls=%fused_computation.5 | loop fusion | flops 2097152 | bytes 16793600 | tf_op jit(solution)/shard_map/jvp(jit(_where))/select_n | solution.py:40
  264.7 9.3 %copy.181 = f32[128,128,128]{1,0,2:T(8,128)} copy(f32[128,128,128]{2,1,0:T(8,128)} %broadcast_select_fusion) | data formatting | bytes 16777216 | tf_op jit(solution)/shard_map/jvp(jit(_where))/select_n | solution.py:40
  274.0 10.1 %fusion.9 = bf16[8,128,128]{1,0,2:T(8,128)(2,1)S(1)} fusion(f32[128,8,128]{2,1,0:T(8,128)} %fusion.13, f32[128,128,128]{1,0,2:T(8,128)} %copy.181, bf16[128,8,128]{0,2,1:T(8,128)(2,1)} %all-to-all-done), kind=kOutput, calls=%fused_computation.27 | convolution fusion | flops 201588736 | bytes 9437184 | tf_op jit(solution)/shard_map/jvp(ijc,bjc->bic)/dot_general | solution.py:58
  284.2 12.0 %all_to_all.43 = bf16[8,128,128]{1,2,0:T(8,128)(2,1)S(1)} all-to-all(bf16[8,128,128]{1,2,0:T(8,128)(2,1)S(1)} %copy.185), channel_id=1, replica_groups=mesh['ctx'=8,'tp'=4] {'ctx'}, dimensions={0} | all-to-all | bytes 524288 | tf_op jit(solution)/shard_map/all_to_all | solution.py:72
  297.0 2.0 copy.208
  299.0 17.4 %convolution_bitcast_fusion = f32[8192,1024]{0,1:T(8,128)} fusion(bf16[128,8192]{1,0:T(8,128)(2,1)} %all-gather.2.cloned.1.call-done, f32[128,1024]{1,0:T(8,128)} %copy.208, f32[128,3,1024]{2,0,1:T(8,128)S(1)} %multiply_add_fusion), kind=kOutput, calls=%fused_computation.3 | convolution fusion | flops 2147745792 | bytes 36700160 | tf_op jit(solution)/shard_map/dot_general | solution.py:98
  317.1 1.3 split.21
  319.8 1.4 multiply_add_fusion.2
  321.9 1.2 pad.127
  323.1 1.9 pad.133
  325.0 1.9 pad.134
  326.9 1.4 multiply_add_fusion.1
  328.4 1.8 pad.128
  330.2 1.8 pad.129
  332.0 1.4 pad.135
  333.5 2.6 pad.113
  336.1 1.5 add_bitcast_fusion
  337.7 1.8 copy.190
  339.5 3.3 fusion.5
  348.2 1.1 collective-permute-start.2
  349.9 2.2 fusion.15
  352.1 7.6 fusion.8
  359.7 32.2 %all_gather.7 = f32[16,1024]{1,0:T(8,128)S(1)} all-gather(f32[16,128]{1,0:T(8,128)S(1)} %fusion.48), channel_id=1, replica_groups=mesh['ctx'=8,'tp'=4] {'ctx'}, dimensions={1}, use_global_device_ids=true | all-gather | bytes 73728 | tf_op jit(solution)/shard_map/all_gather | solution.py:114
  392.7 5.0 all-to-all-start.3
  397.8 2.0 collective-permute-start.3
  399.8 11.2 %collective-permute-done.3 = f32[16,128]{1,0:T(8,128)S(1)} collective-permute-done((f32[16,128]{1,0:T(8,128)S(1)}, f32[16,128]{1,0:T(8,128)S(1)}, u32[]{:S(2)}, u32[]{:S(2)}) %collective-permute-start.3) | collective-permute-done | bytes 8224 | tf_op jit(solution)/shard_map/ppermute | solution.py:18
  411.0 6.8 collective-permute-done.4
  417.8 6.7 collective-permute-done.5
  424.5 6.7 collective-permute-done.6
  431.1 6.6 collective-permute-done.7
  437.8 6.5 collective-permute-done.8
  445.0 1.8 convert_element_type.104
  446.8 2.0 copy.210
  448.8 1.3 multiply_bitcast_fusion
  450.4 1.4 collective-permute-start.1
  452.5 3.8 collective-permute-done.1
  456.5 1.9 multiply_reduce_fusion.2
  458.5 36.6 %psum.7 = f32[3,3,1024]{2,1,0:T(4,128)} all-reduce(f32[3,3,1024]{2,1,0:T(4,128)S(1)} %pad_maximum_fusion.2), channel_id=1, replica_groups=mesh['ctx'=8,'tp'=4] {'ctx'}, use_global_device_ids=true, to_apply=%region_4.5 | all-reduce | flops 9216 | bytes 73728 | tf_op jit(solution)/shard_map/psum | solution.py:135
  495.1 371.5 %reduce-scatter.2.cloned.1.call-done = f32[1024,1024]{0,1:T(8,128)} async-done(((f32[8192,1024]{0,1:T(8,128)}), f32[1024,1024]{0,1:T(8,128)}) %reduce-scatter.2.cloned.1.call-update) | async-done | bytes 4194320 | tf_op jit(solution)/shard_map/reduce_scatter | solution.py:97
  866.6 5.3 copy.206
  (115 shorter events, 26.4 us)
Async XLA Ops:
  7.2 31.6 %all-gather.2.cloned.1.call-start = ((), (), s32[]{:S(2)}) async-start(), calls=%async_computation.5 | async-start | bytes 2621440 | tf_op jit(solution)/shard_map/all_gather | solution.py:96
  8.7 7.7 collective-permute-start
  13.6 21.0 %copy-start.16 = (f32[128]{0:T(128)}, f32[128]{0:T(128)S(1)}, u32[]{:S(2)}) copy-start(f32[128]{0:T(128)S(1)} %broadcast_subtract_fusion) | copy-start | bytes 1540
  15.0 23.7 %copy-start.13 = (f32[16,128]{1,0:T(8,128)}, f32[16,128]{1,0:T(8,128)S(1)}, u32[]{:S(2)}) copy-start(f32[16,128]{1,0:T(8,128)S(1)} %get-tuple-element.58) | copy-start | bytes 24580
  15.8 2.5 copy-start.3
  15.8 2.5 copy-start.5
  15.8 2.5 copy-start.7
  20.8 13.8 %all-to-all-start = ((bf16[128,8,128]{0,2,1:T(8,128)(2,1)}), bf16[128,8,128]{0,2,1:T(8,128)(2,1)}, u32[]{:S(2)}, u32[]{:S(2)}) async-start(bf16[128,8,128]{0,2,1:T(8,128)(2,1)} %bitcast.111), calls=%async_computation | async-start | bytes 524288 | tf_op jit(solution)/shard_map/all_to_all | solution.py:68
  38.7 19.2 %copy-start.14 = (f32[2,16,128]{2,1,0:T(8,128)}, f32[2,16,128]{2,1,0:T(8,128)S(1)}, u32[]{:S(2)}) copy-start(f32[2,16,128]{2,1,0:T(8,128)S(1)} %slice_add_fusion.3) | copy-start | bytes 49156
  53.5 12.3 %all-to-all-start.2 = ((bf16[128,8,128]{0,2,1:T(8,128)(2,1)}), bf16[128,8,128]{0,2,1:T(8,128)(2,1)}, u32[]{:S(2)}, u32[]{:S(2)}) async-start(bf16[128,8,128]{0,2,1:T(8,128)(2,1)} %bitcast.110), calls=%async_computation.2 | async-start | bytes 524288 | tf_op jit(solution)/shard_map/all_to_all | solution.py:68
  57.5 809.1 %reduce-scatter.2.cloned.1.call-start = ((), (), s32[]{:S(2)}) async-start(), calls=%async_computation.6 | async-start | bytes 37748736 | tf_op jit(solution)/shard_map/reduce_scatter | solution.py:97
  57.9 0.7 copy-start.10
  57.9 0.7 copy-start.12
  71.5 2.0 copy-start.9
  77.1 3.3 copy-start.2
  316.4 1.9 copy-start.15
  316.4 2.0 copy-start.1
  316.4 2.0 copy-start.11
  348.2 49.6 %collective-permute-start.2 = (f32[16,128]{1,0:T(8,128)S(1)}, f32[16,128]{1,0:T(8,128)S(1)}, u32[]{:S(2)}, u32[]{:S(2)}) collective-permute-start(f32[16,128]{1,0:T(8,128)S(1)} %get-tuple-element.52), channel_id=1, source_target_pairs={{0,4},{4,8},{8,12},{12,16},{16,20},{20,24},{24,28},{28,0},{1,5},{5... | collective-permute-start | bytes 24584 | tf_op jit(solution)/shard_map/ppermute | solution.py:18
  392.7 52.2 %all-to-all-start.3 = ((bf16[8,128,128]{1,2,0:T(8,128)(2,1)}), bf16[8,128,128]{1,2,0:T(8,128)(2,1)}, u32[]{:S(2)}, u32[]{:S(2)}) async-start(bf16[8,128,128]{1,2,0:T(8,128)(2,1)} %copy.192), calls=%async_computation.3 | async-start | bytes 524288 | tf_op jit(solution)/shard_map/all_to_all | solution.py:72
  397.8 13.2 %collective-permute-start.3 = (f32[16,128]{1,0:T(8,128)S(1)}, f32[16,128]{1,0:T(8,128)S(1)}, u32[]{:S(2)}, u32[]{:S(2)}) collective-permute-start(f32[16,128]{1,0:T(8,128)S(1)} %collective-permute-done.2), channel_id=1, source_target_pairs={{0,4},{4,8},{8,12},{12,16},{16,20},{20,24},{24,28},{28,0},{1,5},{5... | collective-permute-start | bytes 24584 | tf_op jit(solution)/shard_map/ppermute | solution.py:18
  411.0 6.8 collective-permute-start.4
  417.8 6.7 collective-permute-start.5
  424.4 6.7 collective-permute-start.6
  431.1 6.7 collective-permute-start.7
  437.8 6.5 collective-permute-start.8
  448.8 1.4 copy-start
  450.4 6.1 copy-start.4
  450.4 6.1 copy-start.6
  450.4 6.1 copy-start.8
  450.4 5.9 collective-permute-start.1
Sparse Core Ops, SparseCore 0:
  9.6 25.2 all-gather.1
  316.6 549.9 reduce-scatter.1
